TPU v7x, 32 devices: a whole 2x2x4 slice. The times are simulated.
32 devices in a mesh: lat: 8 (over z, x), lev: 4 (over y, core).
Axes of the slice: x: 2, y: 2, z: 4, core: 2. Of those that a mesh axis runs over, the one named last changes fastest.
Arguments:
- fields: float32 [2, 32, 64, 3072], P(None, 'lat', 'lev'), may hold values from -6 to 6
- courant: bfloat16 [2, 32, 64, 3072], P(None, 'lat', 'lev'), may hold values from -0.3984375 to 0.3984375
- cutoffs: int32 [32], replicated, may hold values from 1 to 1536, as said below
- surface: float32 [32, 3072], P('lat'), may hold values from -6 to 6
- remap_weights: float32 [64, 64], replicated, may hold values from -0.25 to 0.75
Outputs:
- remapped: float32 [2, 32, 64, 3072], P(None, 'lat', None, 'lev')
- geopotential: float32 [32, 64, 3072], P('lat', None, 'lev')
Inputs may be any that keep to these rules, and one draw needn't show every extreme that they name: cutoffs[j] is 1536 except on the first and the last 4 latitudes, where it lies between 1 and 127; it equals 127 on some latitude among the first 4.
All inputs are finite; a program needn't handle non-finite values.
Results may differ from a plain program's by a relative error of at most 0.0003.
Values may be sent and summed in bfloat16 or wider, within the bound.
No kernel may reach another device: no remote copies, remote signals or barrier semaphores. Data moves between devices by JAX's collectives and lax.ppermute only.
A program may use at most 64 MiB of HBM per device.

v0:
```python
import functools
import math

import jax
import jax.numpy as jnp
import ml_dtypes
import numpy as np
from jax import lax
from jax.experimental import pallas as pl
from jax.experimental.pallas import tpu as pltpu
from jax.sharding import PartitionSpec as P

KMAX = 128
LANE = 128
TOP = 32767.0
STEPS = 256.0
TINY = 2.0**-100
WIND = 81920.0
ROUND = 1.5 * 2.0**23
VMEM_LIMIT = 48 * 2**20


def rounded(values):
    return ((values + ROUND) - ROUND).astype(jnp.int32).astype(jnp.int16)


def lane_max(values):
    chunks = [jnp.abs(values[:, i : i + LANE]) for i in range(0, values.shape[1], LANE)]
    while len(chunks) > 1:
        pairs = [jnp.maximum(a, b) for a, b in zip(chunks[0::2], chunks[1::2])]
        chunks = pairs + chunks[2 * len(pairs) :]
    return chunks[0]


def tiled(tile, width):
    return jnp.concatenate([tile] * (width // LANE), axis=1)


def scale_code(largest):
    return jnp.ceil(jnp.log2(jnp.maximum(largest, TINY)) * STEPS)


def encoder(code):
    return TOP / jnp.exp2(code * (1.0 / STEPS))


def decoder(code16):
    code = code16.astype(jnp.int32).astype(jnp.float32)
    return jnp.exp2(code * (1.0 / STEPS)) * (1.0 / TOP)


def encode_row(values, out_ref, at):
    width = values.shape[1]
    code = scale_code(lane_max(values))
    out_ref[:, at : at + width] = rounded(values * tiled(encoder(code), width))
    out_ref[:, at + width : at + width + LANE] = code.astype(jnp.int32).astype(jnp.int16)


def decode_row(in_ref, at, width):
    scale = decoder(in_ref[:, at + width : at + width + LANE])
    values = in_ref[:, at : at + width].astype(jnp.int32).astype(jnp.float32)
    return values * tiled(scale, width)


def wind_codes(east, north):
    return rounded(jnp.concatenate([east, north], axis=0) * WIND)


class Sizes:
    def __init__(self, rows, levels, lon):
        self.rows, self.levels, self.lon = rows, levels, lon
        self.half = levels // 2
        self.band = 2 * rows
        self.pad = lon + 2 * LANE
        self.code = lon + LANE
        self.edge = 2 * self.code + lon
        self.inner = 2 * self.code + 3 * lon


def put_padded(ref, index, values, lon):
    ref[index + (Ellipsis, slice(LANE, LANE + lon))] = values
    ref[index + (Ellipsis, slice(0, LANE))] = values[..., lon - LANE :]
    ref[index + (Ellipsis, slice(LANE + lon, 2 * LANE + lon))] = values[..., :LANE]


def pack_kernel(z, par_ref, fields_ref, courant_ref, edge_ref, inner_ref, own_ref):
    p = par_ref[0]
    keep = pl.multiple_of(p * z.half, z.half)
    give = pl.multiple_of((1 - p) * z.half, z.half)

    def field_row(row, start):
        return jnp.concatenate([fields_ref[f, row, pl.ds(start, z.half)] for f in range(2)], axis=0)

    def wind_row(row, upper):
        halves = []
        for k in range(2):
            wind = courant_ref[k, row].astype(jnp.float32)
            halves.append(jnp.where(upper == 1, wind[z.half :], wind[: z.half]))
        return wind_codes(*halves)

    edge, inner = 2 * p, 2 * (1 - p)
    outer = 3 * p
    for r in range(2):
        encode_row(field_row(edge + r, give), edge_ref, r * z.code)
        encode_row(field_row(edge + r, keep), own_ref, r * z.code)
        encode_row(field_row(inner + r, give), inner_ref, r * z.code)
    at = 2 * z.code
    edge_ref[:, at : at + z.lon] = wind_row(outer, 1 - p)
    own_ref[:, at : at + z.lon] = wind_row(outer, p)
    for i, row in enumerate((inner, inner + 1, 1 + p)):
        inner_ref[:, at + i * z.lon : at + (i + 1) * z.lon] = wind_row(row, 1 - p)


def substep(z, u_ref, fwx_ref, fwy_ref, write):
    width = next(w for w in (768, 512, 384, 256, 128) if z.lon % w == 0)
    wide = width + 2 * LANE

    def part(i, carry):
        at = pl.multiple_of(i * width, LANE)
        mid = pl.multiple_of(at + LANE, LANE)
        for f in range(2):

            def middle(j):
                return u_ref[j, f, :, pl.ds(mid, width)]

            rows = [middle(j) for j in range(4)]
            sums = [rows[0] + rows[1], rows[1] + rows[2], rows[2] + rows[3]]
            flux = None
            for j in range(z.band + 1):
                face = fwy_ref[j, :, pl.ds(at, width)]
                new = face * (8.0 * sums[1] - (sums[0] + sums[2]))
                if j > 0:
                    u = u_ref[j + 1, f, :, pl.ds(at, wide)]
                    pair = u + pltpu.roll(u, wide - 1, 1)
                    high = pltpu.roll(pair, wide - 1, 1)
                    low = pltpu.roll(pair, 1, 1)
                    fx = fwx_ref[j - 1, :, pl.ds(at, wide)] * (8.0 * pair - (low + high))
                    change = fx - pltpu.roll(fx, 1, 1)
                    out = u[:, LANE : LANE + width] - change[:, LANE : LANE + width] - (new - flux)
                    write(j - 1, f, at, width, out)
                flux = new
                if j < z.band:
                    above = middle(j + 4)
                    rows = rows[1:] + [above]
                    sums = sums[1:] + [rows[2] + rows[3]]
        return carry

    lax.fori_loop(0, z.lon // width, part, 0)


def filter_tables(lon):
    points = np.arange(lon // 2)
    forward, back = [], []
    for parity in range(2):
        waves = np.arange(parity, KMAX, 2)
        angle = (points[:, None] * waves[None, :] % lon) * (2.0 * math.pi / lon)
        table = np.concatenate([np.cos(angle), np.sin(angle)], axis=1).astype(np.float32)
        high = table.astype(ml_dtypes.bfloat16)
        low = (table - high.astype(np.float32)).astype(ml_dtypes.bfloat16)
        forward.append(np.concatenate([high, low], axis=1))
        back.append(np.concatenate([high.T, low.T], axis=0))
    return np.stack(forward), np.stack(back)


def split(values):
    high = values.astype(jnp.bfloat16)
    return high, (values - high.astype(jnp.float32)).astype(jnp.bfloat16)


def low_pass(z, rows, cuts, forward_ref, back_ref):
    half = z.lon // 2
    count = len(rows)
    tall = 2 * z.half
    total = count * tall
    flat = [row.reshape(tall, z.lon) for row in rows]
    folded = []
    for parity in range(2):
        parts = [
            row[:, :half] + row[:, half:] if parity == 0 else row[:, :half] - row[:, half:]
            for row in flat
        ]
        high, low = split(jnp.concatenate(parts, axis=0))
        both = jnp.concatenate([high, low], axis=0)
        got = jnp.dot(both, forward_ref[parity], preferred_element_type=jnp.float32)
        wave = got[:total, :KMAX] + got[:total, KMAX:] + (got[total:, :KMAX] + got[total:, KMAX:])
        number = 2 * (lax.broadcasted_iota(jnp.int32, (tall, KMAX), 1) % (KMAX // 2)) + parity
        doubled = jnp.where(number == 0, 1.0, 2.0) * (1.0 / z.lon)
        weight = jnp.concatenate([jnp.where(number <= cut, doubled, 0.0) for cut in cuts], axis=0)
        high, low = split(wave * weight)
        both = jnp.concatenate(
            [jnp.concatenate([high, high], axis=1), jnp.concatenate([low, low], axis=1)], axis=0
        )
        got = jnp.dot(both, back_ref[parity], preferred_element_type=jnp.float32)
        folded.append(got[:total] + got[total:])
    left, right = folded[0] + folded[1], folded[0] - folded[1]
    smooth = jnp.concatenate([left, right], axis=1)
    return [smooth[i * tall : (i + 1) * tall].reshape(2, z.half, z.lon) for i in range(count)]


def filter_band(z, cut_ref, first_row, forward_ref, back_ref, load, store):
    nyquist = z.lon // 2
    for part in range(2):
        start = part * z.rows
        cuts = [cut_ref[first_row + start + r] for r in range(z.rows)]
        some = functools.reduce(jnp.logical_or, [cut < nyquist for cut in cuts])

        @pl.when(some)
        def _():
            rows = [load(start + r) for r in range(z.rows)]
            smooth = low_pass(z, rows, cuts, forward_ref, back_ref)
            for r in range(z.rows):

                @pl.when(cuts[r] < nyquist)
                def _():
                    store(start + r, smooth[r])


def first_kernel(
    z, par_ref, fields_ref, courant_ref, edge_ref, inner_ref, near_ref, far_ref,
    new_ref, fwx_ref, fwy_ref, down_ref, up_ref, u_ref, cx_ref, cy_ref,
):
    p = par_ref[0]
    lon, half = z.lon, z.half

    def pair(values):
        return values.reshape(2, half, values.shape[1])

    def winds(in_ref, at):
        values = in_ref[:, at : at + lon].astype(jnp.int32).astype(jnp.float32) * (1.0 / WIND)
        return values[:half], values[half:]

    def place_wind(row, east, north):
        put_padded(cx_ref, (row,), east, lon)
        cy_ref[row + 1] = north

    keep = pl.multiple_of(p * half, half)
    for r in range(z.rows):
        row = z.rows * p + r
        own = jnp.stack([fields_ref[f, r, pl.ds(keep, half)] for f in range(2)])
        put_padded(u_ref, (row + 2,), own, lon)
        got = []
        for k in range(2):
            wind = courant_ref[k, r].astype(jnp.float32)
            got.append(jnp.where(p == 1, wind[half:], wind[:half]))
        place_wind(row, *got)
    at = 2 * z.code
    for r in range(2):
        put_padded(u_ref, (6 * (1 - p) + r + 2,), pair(decode_row(edge_ref, r * z.code, lon)), lon)
        put_padded(u_ref, (4 - 2 * p + r + 2,), pair(decode_row(inner_ref, r * z.code, lon)), lon)
        put_padded(u_ref, (10 * (1 - p) + r,), pair(decode_row(near_ref, r * z.code, lon)), lon)
        put_padded(u_ref, (10 * p + r,), pair(decode_row(far_ref, r * z.code, lon)), lon)
        place_wind(4 - 2 * p + r, *winds(inner_ref, at + r * lon))
    place_wind(7 * (1 - p), *winds(edge_ref, at))
    place_wind(6 - 5 * p, *winds(inner_ref, at + 2 * lon))
    cy_ref[9 * (1 - p)] = winds(near_ref, at)[1]
    cy_ref[9 * p] = winds(far_ref, at)[1]

    def face_rows(j, carry):
        wind = cx_ref[j]
        fwx_ref[j] = (wind + pltpu.roll(wind, z.pad - 1, 1)) * (1.0 / 24.0)
        return carry

    lax.fori_loop(0, z.band, face_rows, 0)

    def face_cols(j, carry):
        fwy_ref[j] = (cy_ref[j] + cy_ref[j + 1]) * (1.0 / 24.0)
        return carry

    lax.fori_loop(0, z.band + 1, face_cols, 0)

    def write(row, f, at, width, values):
        new_ref[row, f, :, pl.ds(pl.multiple_of(at + LANE, LANE), width)] = values

    substep(z, u_ref, fwx_ref, fwy_ref, write)
    for r in range(2):
        for row, out_ref in ((r, down_ref), (z.band - 2 + r, up_ref)):
            values = new_ref[row, :, :, LANE : LANE + lon]
            encode_row(values.reshape(2 * half, lon), out_ref, r * z.code)

    def wrap(j, carry):
        new_ref[j, :, :, 0:LANE] = new_ref[j, :, :, lon : lon + LANE]
        new_ref[j, :, :, LANE + lon :] = new_ref[j, :, :, LANE : 2 * LANE]
        return carry

    lax.fori_loop(0, z.band, wrap, 0)


def filter_kernel(z, par_ref, cut_ref, forward_ref, back_ref, new_in_ref, new_ref):
    del new_in_ref
    first_row = par_ref[1]

    def store(row, values):
        put_padded(new_ref, (row,), values, z.lon)

    filter_band(
        z, cut_ref, first_row, forward_ref, back_ref,
        lambda row: new_ref[row, :, :, LANE : LANE + z.lon], store,
    )


def second_kernel(
    z, parts, par_ref, cut_ref, new_ref, fwx_ref, fwy_ref, below_ref, above_ref, forward_ref,
    back_ref, out_ref, u_ref, v_ref,
):
    first_row = par_ref[1]
    lon, half = z.lon, z.half
    tall = 2 * half
    for r in range(2):
        for row, in_ref in ((r, below_ref), (z.band + 2 + r, above_ref)):
            values = decode_row(in_ref, r * z.code, lon).reshape(2, half, lon)
            put_padded(u_ref, (row,), values, lon)

    def copy(j, carry):
        u_ref[j + 2] = new_ref[j]
        return carry

    lax.fori_loop(0, z.band, copy, 0)

    def write(row, f, at, width, values):
        v_ref[row, f, :, pl.ds(at, width)] = values

    substep(z, u_ref, fwx_ref, fwy_ref, write)

    def store(row, values):
        v_ref[row] = values

    filter_band(
        z, cut_ref, first_row, forward_ref, back_ref, lambda row: v_ref[row], store
    )
    column = lon // parts
    for side in range(2):
        for d in range(parts):
            values = jnp.concatenate(
                [
                    v_ref[side * z.rows + r, :, :, d * column : (d + 1) * column].reshape(tall, column)
                    for r in range(z.rows)
                ],
                axis=1,
            )
            encode_row(values, out_ref.at[side * parts + d], 0)


def column_kernel(z, parts, par_ref, got_ref, remap_ref, upward_ref, surface_ref, out_ref, geo_ref):
    r = pl.program_id(0)
    column = out_ref.shape[-1]
    count = 2 * parts
    at = pl.multiple_of(r * column, LANE)
    tiles = []
    for s in range(parts):
        for side in range(2):
            i = side * parts + s
            scale = decoder(got_ref[i, :, z.rows * column : z.rows * column + LANE])
            codes = got_ref[i, :, pl.ds(at, column)].astype(jnp.int32).astype(jnp.float32)
            tiles.append(codes * tiled(scale, column))
    high, low = split(remap_ref[...])
    remap = jnp.concatenate([high, low, high], axis=1)
    for f in range(2):
        values = jnp.concatenate([t[f * z.half : (f + 1) * z.half] for t in tiles], axis=0)
        high, low = split(values)
        stacked = jnp.concatenate([high, high, low], axis=0)
        out_ref[f, 0] = jnp.dot(remap, stacked, preferred_element_type=jnp.float32)
        if f == 1:
            upward = jnp.dot(upward_ref[...], stacked, preferred_element_type=jnp.float32)
            surface = surface_ref[0]
            geo_ref[0] = surface + upward * (out_ref.shape[2] ** -0.5)


def whole():
    return pl.BlockSpec(memory_space=pltpu.VMEM)


def scalars():
    return pl.BlockSpec(memory_space=pltpu.SMEM)


def params():
    return pltpu.CompilerParams(vmem_limit_bytes=VMEM_LIMIT)


def cost(flops, data):
    return pl.CostEstimate(flops=flops, bytes_accessed=data, transcendentals=0)


def shards(fields, courant, cutoffs, surface, remap_weights):
    _, rows, levels, lon = fields.shape
    z = Sizes(rows, levels, lon)
    lats, parts = lax.axis_size("lat"), lax.axis_size("lev")
    me = lax.axis_index("lat")
    parity = me % 2
    place = jnp.stack([parity, (me - parity) * rows]).astype(jnp.int32)
    tall = 2 * z.half
    i16, f32 = jnp.int16, jnp.float32
    swap = [(i, i ^ 1) for i in range(lats)]
    rising = [(i, i + 2) for i in range(lats - 2)]
    falling = [(i + 2, i) for i in range(lats - 2)]
    near_pairs = [(i, j) for i, j in rising if i % 2 == 1] + [(i, j) for i, j in falling if i % 2 == 0]
    far_pairs = [(i, j) for i, j in rising if i % 2 == 0] + [(i, j) for i, j in falling if i % 2 == 1]

    edge, inner, own = pl.pallas_call(
        functools.partial(pack_kernel, z),
        name="pack",
        in_specs=[scalars(), whole(), whole()],
        out_specs=[whole()] * 3,
        out_shape=[
            jax.ShapeDtypeStruct((tall, z.edge), i16),
            jax.ShapeDtypeStruct((tall, z.inner), i16),
            jax.ShapeDtypeStruct((tall, z.edge), i16),
        ],
        compiler_params=params(),
        cost_estimate=cost(10**7, 5 * 10**6),
    )(place, fields, courant)
    edge = lax.ppermute(edge, "lat", swap)
    near = lax.ppermute(own, "lat", near_pairs)
    inner = lax.ppermute(inner, "lat", swap)
    far = lax.ppermute(edge, "lat", far_pairs)

    new, fwx, fwy, down, up = pl.pallas_call(
        functools.partial(first_kernel, z),
        name="first",
        in_specs=[scalars()] + [whole()] * 6,
        out_specs=[whole()] * 5,
        out_shape=[
            jax.ShapeDtypeStruct((z.band, 2, z.half, z.pad), f32),
            jax.ShapeDtypeStruct((z.band, z.half, z.pad), f32),
            jax.ShapeDtypeStruct((z.band + 1, z.half, z.lon), f32),
            jax.ShapeDtypeStruct((tall, 2 * z.code), i16),
            jax.ShapeDtypeStruct((tall, 2 * z.code), i16),
        ],
        scratch_shapes=[
            pltpu.VMEM((z.band + 4, 2, z.half, z.pad), f32),
            pltpu.VMEM((z.band, z.half, z.pad), f32),
            pltpu.VMEM((z.band + 2, z.half, z.lon), f32),
        ],
        compiler_params=params(),
        cost_estimate=cost(4 * 10**7, 8 * 10**6),
    )(place, fields, courant, edge, inner, near, far)
    above = lax.ppermute(down, "lat", falling)
    below = lax.ppermute(up, "lat", rising)

    forward, back = (jnp.asarray(t) for t in filter_tables(lon))
    new = pl.pallas_call(
        functools.partial(filter_kernel, z),
        name="smooth",
        in_specs=[scalars(), scalars()] + [whole()] * 3,
        out_specs=whole(),
        out_shape=jax.ShapeDtypeStruct(new.shape, f32),
        input_output_aliases={4: 0},
        compiler_params=params(),
        cost_estimate=cost(10**9, 6 * 10**6),
    )(place, cutoffs, forward, back, new)

    column = lon // parts
    codes = pl.pallas_call(
        functools.partial(second_kernel, z, parts),
        name="second",
        in_specs=[scalars(), scalars()] + [whole()] * 7,
        out_specs=whole(),
        out_shape=jax.ShapeDtypeStruct((2 * parts, tall, rows * column + LANE), i16),
        scratch_shapes=[
            pltpu.VMEM((z.band + 4, 2, z.half, z.pad), f32),
            pltpu.VMEM((z.band, 2, z.half, lon), f32),
        ],
        compiler_params=params(),
        cost_estimate=cost(10**9, 8 * 10**6),
    )(place, cutoffs, new, fwx, fwy, below, above, forward, back)
    groups = [[i * parts + j for i in (a, a + 1) for j in range(parts)] for a in range(0, lats, 2)]
    got = lax.all_to_all(codes, ("lat", "lev"), 0, 0, axis_index_groups=groups, tiled=True)

    count = remap_weights.shape[0]
    upward = np.triu(np.ones((count, count), np.float32), 1) + 0.5 * np.eye(count, dtype=np.float32)
    upward = jnp.asarray(
        np.concatenate([upward, 0.0 * upward, upward], axis=1).astype(ml_dtypes.bfloat16)
    )
    mine = lax.dynamic_slice_in_dim(surface, lax.axis_index("lev") * column, column, 1)
    remapped, geopotential = pl.pallas_call(
        functools.partial(column_kernel, z, parts),
        name="columns",
        grid=(rows,),
        in_specs=[
            scalars(),
            pl.BlockSpec(got.shape, lambda r: (0, 0, 0)),
            pl.BlockSpec(remap_weights.shape, lambda r: (0, 0)),
            pl.BlockSpec(upward.shape, lambda r: (0, 0)),
            pl.BlockSpec((1, 1, column), lambda r: (r, 0, 0)),
        ],
        out_specs=[
            pl.BlockSpec((2, 1, count, column), lambda r: (0, r, 0, 0)),
            pl.BlockSpec((1, count, column), lambda r: (r, 0, 0)),
        ],
        out_shape=[
            jax.ShapeDtypeStruct((2, rows, count, column), f32),
            jax.ShapeDtypeStruct((rows, count, column), f32),
        ],
        compiler_params=params(),
        cost_estimate=cost(10**8, 4 * 10**6),
    )(place, got, remap_weights, upward, mine[:, None, :])
    return remapped, geopotential


def with_halo(shard, width):
    size, length = lax.axis_size("lat"), shard.shape[1]
    up = [(i, (i + 1) % size) for i in range(size - 1)]
    down = [(j, i) for i, j in up]
    before = lax.ppermute(lax.slice_in_dim(shard, length - width, length, axis=1), "lat", up)
    after = lax.ppermute(lax.slice_in_dim(shard, 0, width, axis=1), "lat", down)
    return jnp.concatenate([before, shard, after], axis=1)


def plain_shards(fields, courant, cutoffs, surface, remap_weights):
    _, rows, _, lon = fields.shape
    exact = lax.Precision.HIGHEST
    cut = lax.dynamic_slice_in_dim(cutoffs, lax.axis_index("lat") * rows, rows)
    waves = np.arange(KMAX)
    angle = (np.arange(lon)[:, None] * waves[None, :] % lon) * (2.0 * math.pi / lon)
    table = jnp.asarray(np.concatenate([np.cos(angle), np.sin(angle)], axis=1).astype(np.float32))
    number = jnp.asarray(np.concatenate([waves, waves]).astype(np.int32))
    weight = jnp.where(number[None] <= cut[:, None], jnp.where(number == 0, 1.0, 2.0)[None] / lon, 0.0)
    flagged = cut < lon // 2

    def smooth(values):
        wave = jnp.einsum("frln,nk->frlk", values, table, precision=exact) * weight[None, :, None]
        low = jnp.einsum("frlk,nk->frln", wave, table, precision=exact)
        return jnp.where(flagged[None, :, None, None], low, values)

    winds = with_halo(courant, 1).astype(jnp.float32)
    east, north = winds[0, 1:-1], winds[1]
    face_x = (east + jnp.roll(east, -1, -1)) / 24.0
    face_y = (north[:-1] + north[1:]) / 24.0
    u = fields
    for _ in range(2):
        wide = with_halo(u, 2)
        pair = u + jnp.roll(u, -1, -1)
        fx = face_x * (8.0 * pair - (jnp.roll(pair, 1, -1) + jnp.roll(pair, -1, -1)))
        pair = wide[:, :-1] + wide[:, 1:]
        fy = face_y * (8.0 * pair[:, 1:-1] - (pair[:, :-2] + pair[:, 2:]))
        u = u - (fx - jnp.roll(fx, 1, -1)) - (fy[:, 1:] - fy[:, :-1])
        u = lax.cond(jnp.any(flagged), smooth, lambda values: values, u)
    columns = lax.all_to_all(u, "lev", split_axis=3, concat_axis=2, tiled=True)
    remapped = jnp.einsum("pk,fjkn->fjpn", remap_weights, columns, precision=exact)
    count = remap_weights.shape[0]
    upward = np.triu(np.ones((count, count), np.float32), 1) + 0.5 * np.eye(count, dtype=np.float32)
    upward = jnp.einsum("kl,jln->jkn", jnp.asarray(upward), columns[1], precision=exact)
    width = lon // lax.axis_size("lev")
    mine = lax.dynamic_slice_in_dim(surface, lax.axis_index("lev") * width, width, 1)
    return remapped, mine[:, None] + count**-0.5 * upward


def solution(mesh):
    def program(fields, courant, cutoffs, surface, remap_weights):
        lats, parts = mesh.shape["lat"], mesh.shape["lev"]
        rows, levels = fields.shape[1] // lats, fields.shape[2] // parts
        polar = fields.shape[1] // 8
        paired = (
            lats % 2 == 0
            and rows == 4
            and levels % 16 == 0
            and polar <= 2 * rows - 2
            and fields.shape[3] % (LANE * parts) == 0
        )
        return jax.shard_map(
            shards if paired else plain_shards,
            mesh=mesh,
            in_specs=(
                P(None, "lat", "lev", None),
                P(None, "lat", "lev", None),
                P(),
                P("lat", None),
                P(),
            ),
            out_specs=(P(None, "lat", None, "lev"), P("lat", None, "lev")),
            check_vma=False,
        )(fields, courant, cutoffs, surface, remap_weights)

    return program
```

profile of v0, /device:TPU:0, one launch (start us, length us, event | category | flops | bytes accessed | tf_op | source)
XLA Modules:
  0.0 78.5 jit_solution(4680755777640463267)
XLA Ops:
  0.6 0.0 copy-start
  0.7 0.1 pad_add_fusion.par_ref
  0.7 0.0 copy-start.3
  0.7 1.4 %copy-done.3 = f32[2,4,16,3072]{3,2,1,0:T(8,128)S(1)} copy-done((f32[2,4,16,3072]{3,2,1,0:T(8,128)S(1)}, f32[2,4,16,3072]{3,2,1,0:T(8,128)}, u32[]{:S(2)}) %copy-start.3) | copy-done | bytes 1572888
  2.1 0.0 copy-start.6
  2.1 1.1 %copy-done.6 = bf16[2,4,16,3072]{3,2,1,0:T(8,128)(2,1)S(1)} copy-done((bf16[2,4,16,3072]{3,2,1,0:T(8,128)(2,1)S(1)}, bf16[2,4,16,3072]{3,2,1,0:T(8,128)(2,1)}, u32[]{:S(2)}) %copy-start.6) | copy-done | bytes 786456
  3.3 1.1 %pack.1 = (s16[16,9472]{1,0:T(8,128)(2,1)S(1)}, s16[16,15616]{1,0:T(8,128)(2,1)S(1)}, s16[16,9472]{1,0:T(8,128)(2,1)S(1)}) custom-call(s32[2]{0:T(128)S(1)} %pad_add_fusion.par_ref, f32[2,4,16,3072]{3,2,1,0:T(8,128)S(1)} %copy-done.3, bf16[2,4,16,3072]{3,2,1,0:T(8,128)(2,1)S(1)} %copy-done.6), custom_call_target="tpu_custom_call" | custom-call | flops 10000000 | bytes 5000000 | tf_op jit(solution)/shard_map/pack/pallas_call | solution.py:399
  4.4 3.0 %collective-permute-start = (s16[16,9472]{1,0:T(8,128)(2,1)S(1)}, s16[16,9472]{1,0:T(8,128)(2,1)S(1)}, u32[]{:S(2)}, u32[]{:S(2)}) collective-permute-start(s16[16,9472]{1,0:T(8,128)(2,1)S(1)} %get-tuple-element.10), channel_id=1, source_target_pairs={{0,4},{4,0},{8,12},{12,8},{16,20},{20,16},{24,28},{28,24},{1,5},{5... | collective-permute-start | bytes 909320 | tf_op jit(solution)/shard_map/ppermute | solution.py:412
  7.4 0.1 collective-permute-start.1
  7.5 0.0 copy-start.4
  7.5 0.0 copy-start.5
  7.5 0.0 copy-start.9
  7.5 1.5 %collective-permute-start.2 = (s16[16,9472]{1,0:T(8,128)(2,1)S(1)}, s16[16,9472]{1,0:T(8,128)(2,1)S(1)}, u32[]{:S(2)}, u32[]{:S(2)}) collective-permute-start(s16[16,9472]{1,0:T(8,128)(2,1)S(1)} %get-tuple-element.12), channel_id=1, source_target_pairs={{4,12},{12,20},{20,28},{8,0},{16,8},{24,16},{5,13},{13,21},{21,29}... | collective-permute-start | bytes 909320 | tf_op jit(solution)/shard_map/ppermute | solution.py:413
  9.0 6.4 %collective-permute-done.edge_ref = s16[16,9472]{1,0:T(8,128)(2,1)S(1)} collective-permute-done((s16[16,9472]{1,0:T(8,128)(2,1)S(1)}, s16[16,9472]{1,0:T(8,128)(2,1)S(1)}, u32[]{:S(2)}, u32[]{:S(2)}) %collective-permute-start) | collective-permute-done | bytes 303136 | tf_op jit(solution)/shard_map/ppermute | solution.py:412
  15.4 4.1 %collective-permute-start.3 = (s16[16,9472]{1,0:T(8,128)(2,1)S(1)}, s16[16,9472]{1,0:T(8,128)(2,1)S(1)}, u32[]{:S(2)}, u32[]{:S(2)}) collective-permute-start(s16[16,9472]{1,0:T(8,128)(2,1)S(1)} %collective-permute-done.edge_ref), channel_id=1, source_target_pairs={{0,8},{8,16},{16,24},{12,4},{20,12},{28,20},{1,9},{9,17},{17,25},{... | collective-permute-start | bytes 909320 | tf_op jit(solution)/shard_map/ppermute | solution.py:415
  19.5 0.0 collective-permute-done.2.near_ref
  19.5 5.8 %collective-permute-done.1.inner_ref = s16[16,15616]{1,0:T(8,128)(2,1)S(1)} collective-permute-done((s16[16,15616]{1,0:T(8,128)(2,1)S(1)}, s16[16,15616]{1,0:T(8,128)(2,1)S(1)}, u32[]{:S(2)}, u32[]{:S(2)}) %collective-permute-start.1) | collective-permute-done | bytes 499744 | tf_op jit(solution)/shard_map/ppermute | solution.py:414
  25.3 0.0 collective-permute-done.3.far_ref
  25.3 11.1 %first.1 = (f32[8,2,8,3328]{3,2,1,0:T(8,128)}, f32[8,8,3328]{2,1,0:T(8,128)S(1)}, f32[9,8,3072]{2,1,0:T(8,128)S(1)}, s16[16,6400]{1,0:T(8,128)(2,1)S(1)}, s16[16,6400]{1,0:T(8,128)(2,1)S(1)}) custom-call(s32[2]{0:T(128)S(1)} %pad_add_fusion.par_ref, f32[2,4,16,3072]{3,2,1,0:T(8,128)S(1)} %copy-done.3, bf16[2,4,16,3072]{3,2,1,0:T(8,128)(2,1)S(1)} %copy-done.6, ...), custom_call_target="tpu_custom_call" | custom-call | flops 40000000 | bytes 8000000 | tf_op jit(solution)/shard_map/first/pallas_call | solution.py:417
  36.4 3.7 %collective-permute-start.4 = (s16[16,6400]{1,0:T(8,128)(2,1)S(1)}, s16[16,6400]{1,0:T(8,128)(2,1)S(1)}, u32[]{:S(2)}, u32[]{:S(2)}) collective-permute-start(s16[16,6400]{1,0:T(8,128)(2,1)S(1)} %get-tuple-element.16), channel_id=1, source_target_pairs={{0,8},{4,12},{8,16},{12,20},{16,24},{20,28},{1,9},{5,13},{9,17},{1... | collective-permute-start | bytes 614408 | tf_op jit(solution)/shard_map/ppermute | solution.py:438
  40.1 1.3 %collective-permute-start.5 = (s16[16,6400]{1,0:T(8,128)(2,1)S(1)}, s16[16,6400]{1,0:T(8,128)(2,1)S(1)}, u32[]{:S(2)}, u32[]{:S(2)}) collective-permute-start(s16[16,6400]{1,0:T(8,128)(2,1)S(1)} %get-tuple-element.17), channel_id=1, source_target_pairs={{8,0},{12,4},{16,8},{20,12},{24,16},{28,20},{9,1},{13,5},{17,9},{2... | collective-permute-start | bytes 614408 | tf_op jit(solution)/shard_map/ppermute | solution.py:437
  41.4 0.0 copy-done.4
  41.4 0.0 copy-done.5
  41.4 0.0 copy-done.9
  41.4 0.0 copy-start.1
  41.4 1.4 %copy-done.1 = f32[8,2,8,3328]{3,2,1,0:T(8,128)S(1)} copy-done((f32[8,2,8,3328]{3,2,1,0:T(8,128)S(1)}, f32[8,2,8,3328]{3,2,1,0:T(8,128)}, u32[]{:S(2)}) %copy-start.1) | copy-done | bytes 1703960
  42.9 1.5 %smooth.1.new_ref = f32[8,2,8,3328]{3,2,1,0:T(8,128)S(1)} custom-call(s32[2]{0:T(128)S(1)} %pad_add_fusion.par_ref, s32[32]{0:T(128)S(1)} %copy-done.9, bf16[2,1536,256]{2,1,0:T(8,128)(2,1)S(1)} %copy-done.4, bf16[2,256,1536]{2,1,0:T(8,128)(2,1)S(1)} %copy-done.5, f32[8,2,8,3328]{3,2,1,0:T(8,128)S(1)} %copy-done.1), custom_call_target="tpu_custom_call", output_to_operand_aliasing={{}: (4, {})} | custom-call | flops 1000000000 | bytes 6000000 | tf_op jit(solution)/shard_map/smooth/pallas_call | solution.py:441
  44.4 0.0 copy-start.2
  44.4 1.2 %copy-done.2 = f32[8,2,8,3328]{3,2,1,0:T(8,128)} copy-done((f32[8,2,8,3328]{3,2,1,0:T(8,128)}, f32[8,2,8,3328]{3,2,1,0:T(8,128)S(1)}, u32[]{:S(2)}) %copy-start.2) | copy-done | bytes 1703960
  45.6 0.0 collective-permute-done.4.below_ref
  45.6 2.1 %collective-permute-done.5.above_ref = s16[16,6400]{1,0:T(8,128)(2,1)S(1)} collective-permute-done((s16[16,6400]{1,0:T(8,128)(2,1)S(1)}, s16[16,6400]{1,0:T(8,128)(2,1)S(1)}, u32[]{:S(2)}, u32[]{:S(2)}) %collective-permute-start.5) | collective-permute-done | bytes 204832 | tf_op jit(solution)/shard_map/ppermute | solution.py:437
  47.7 11.7 %second.1 = s16[8,16,3200]{2,1,0:T(8,128)(2,1)} custom-call(s32[2]{0:T(128)S(1)} %pad_add_fusion.par_ref, s32[32]{0:T(128)S(1)} %copy-done.9, f32[8,2,8,3328]{3,2,1,0:T(8,128)} %copy-done.2, f32[8,8,3328]{2,1,0:T(8,128)S(1)} %get-tuple-element.14.fwx_ref, f32[9,8,3072]{2,1,0:T(8,128)S(1)} %get-tuple-element.15.fwy_ref, ...), custom_call_target="tpu_custom_call" | custom-call | flops 1000000000 | bytes 8000000 | tf_op jit(solution)/shard_map/second/pallas_call | solution.py:453
  59.4 0.0 copy-start.7
  59.4 0.0 copy-start.8
  59.4 3.9 %all-to-all-start = ((s16[8,16,3200]{2,1,0:T(8,128)(2,1)}), s16[8,16,3200]{2,1,0:T(8,128)(2,1)S(1)}, u32[]{:S(2)}, u32[]{:S(2)}) async-start(s16[8,16,3200]{2,1,0:T(8,128)(2,1)} %second.1), calls=%async_computation | async-start | bytes 1638400 | tf_op jit(solution)/shard_map/all_to_all | solution.py:467
  63.3 0.0 copy-done
  63.3 12.0 %all-to-all-done.got_ref = s16[8,16,3200]{2,1,0:T(8,128)(2,1)S(1)} async-done(((s16[8,16,3200]{2,1,0:T(8,128)(2,1)}), s16[8,16,3200]{2,1,0:T(8,128)(2,1)S(1)}, u32[]{:S(2)}, u32[]{:S(2)}) %all-to-all-start) | async-done | bytes 819232 | tf_op jit(solution)/shard_map/all_to_all | solution.py:467
  75.3 0.0 copy-done.7
  75.3 0.0 copy-done.8
  75.3 3.2 %columns.1 = (f32[2,4,64,768]{3,2,1,0:T(8,128)}, f32[4,64,768]{2,1,0:T(8,128)}) custom-call(s32[2]{0:T(128)S(1)} %pad_add_fusion.par_ref, s16[8,16,3200]{2,1,0:T(8,128)(2,1)S(1)} %all-to-all-done.got_ref, f32[64,64]{1,0:T(8,128)S(1)} %copy-done.7, bf16[64,192]{1,0:T(8,128)(2,1)S(1)} %copy-done.8, f32[4,1,768]{2,1,0:T(1,128)S(1)} %broadcast_in_dim.3.surface_ref), custom_call_target="tpu_custom_call" | custom-call | flops 100000000 | bytes 4000000 | tf_op jit(solution)/shard_map/columns/pallas_call | solution.py:475
  (2 shorter events, 0.0 us)
Async XLA Ops:
  0.6 62.7 %copy-start = (f32[4,3072]{1,0:T(4,128)S(1)}, f32[4,3072]{1,0:T(4,128)}, u32[]{:S(2)}) copy-start(f32[4,3072]{1,0:T(4,128)} %param.11) | copy-start | bytes 147460
  0.7 1.4 %copy-start.3 = (f32[2,4,16,3072]{3,2,1,0:T(8,128)S(1)}, f32[2,4,16,3072]{3,2,1,0:T(8,128)}, u32[]{:S(2)}) copy-start(f32[2,4,16,3072]{3,2,1,0:T(8,128)} %fields_ref.3) | copy-start | bytes 4718596
  2.1 1.1 %copy-start.6 = (bf16[2,4,16,3072]{3,2,1,0:T(8,128)(2,1)S(1)}, bf16[2,4,16,3072]{3,2,1,0:T(8,128)(2,1)}, u32[]{:S(2)}) copy-start(bf16[2,4,16,3072]{3,2,1,0:T(8,128)(2,1)} %courant_ref.3) | copy-start | bytes 2359300
  4.4 11.0 %collective-permute-start = (s16[16,9472]{1,0:T(8,128)(2,1)S(1)}, s16[16,9472]{1,0:T(8,128)(2,1)S(1)}, u32[]{:S(2)}, u32[]{:S(2)}) collective-permute-start(s16[16,9472]{1,0:T(8,128)(2,1)S(1)} %get-tuple-element.10), channel_id=1, source_target_pairs={{0,4},{4,0},{8,12},{12,8},{16,20},{20,16},{24,28},{28,24},{1,5},{5... | collective-permute-start | bytes 909320 | tf_op jit(solution)/shard_map/ppermute | solution.py:412
  7.4 17.9 %collective-permute-start.1 = (s16[16,15616]{1,0:T(8,128)(2,1)S(1)}, s16[16,15616]{1,0:T(8,128)(2,1)S(1)}, u32[]{:S(2)}, u32[]{:S(2)}) collective-permute-start(s16[16,15616]{1,0:T(8,128)(2,1)S(1)} %get-tuple-element.11), channel_id=1, source_target_pairs={{0,4},{4,0},{8,12},{12,8},{16,20},{20,16},{24,28},{28,24},{1,5},{5... | collective-permute-start | bytes 1499144 | tf_op jit(solution)/shard_map/ppermute | solution.py:414
  7.5 33.9 %copy-start.4 = (bf16[2,1536,256]{2,1,0:T(8,128)(2,1)S(1)}, bf16[2,1536,256]{2,1,0:T(8,128)(2,1)}, u32[]{:S(2)}) copy-start(bf16[2,1536,256]{2,1,0:T(8,128)(2,1)} %constant.35.clone.forward_ref) | copy-start | bytes 4718596
  7.5 33.9 %copy-start.5 = (bf16[2,256,1536]{2,1,0:T(8,128)(2,1)S(1)}, bf16[2,256,1536]{2,1,0:T(8,128)(2,1)}, u32[]{:S(2)}) copy-start(bf16[2,256,1536]{2,1,0:T(8,128)(2,1)} %constant.36.clone.back_ref) | copy-start | bytes 4718596
  7.5 33.9 %copy-start.9 = (s32[32]{0:T(128)S(1)}, s32[32]{0:T(128)}, u32[]{:S(2)}) copy-start(s32[32]{0:T(128)} %cut_ref.3) | copy-start | bytes 388
  7.5 12.0 %collective-permute-start.2 = (s16[16,9472]{1,0:T(8,128)(2,1)S(1)}, s16[16,9472]{1,0:T(8,128)(2,1)S(1)}, u32[]{:S(2)}, u32[]{:S(2)}) collective-permute-start(s16[16,9472]{1,0:T(8,128)(2,1)S(1)} %get-tuple-element.12), channel_id=1, source_target_pairs={{4,12},{12,20},{20,28},{8,0},{16,8},{24,16},{5,13},{13,21},{21,29}... | collective-permute-start | bytes 909320 | tf_op jit(solution)/shard_map/ppermute | solution.py:413
  15.4 9.9 %collective-permute-start.3 = (s16[16,9472]{1,0:T(8,128)(2,1)S(1)}, s16[16,9472]{1,0:T(8,128)(2,1)S(1)}, u32[]{:S(2)}, u32[]{:S(2)}) collective-permute-start(s16[16,9472]{1,0:T(8,128)(2,1)S(1)} %collective-permute-done.edge_ref), channel_id=1, source_target_pairs={{0,8},{8,16},{16,24},{12,4},{20,12},{28,20},{1,9},{9,17},{17,25},{... | collective-permute-start | bytes 909320 | tf_op jit(solution)/shard_map/ppermute | solution.py:415
  36.4 9.3 %collective-permute-start.4 = (s16[16,6400]{1,0:T(8,128)(2,1)S(1)}, s16[16,6400]{1,0:T(8,128)(2,1)S(1)}, u32[]{:S(2)}, u32[]{:S(2)}) collective-permute-start(s16[16,6400]{1,0:T(8,128)(2,1)S(1)} %get-tuple-element.16), channel_id=1, source_target_pairs={{0,8},{4,12},{8,16},{12,20},{16,24},{20,28},{1,9},{5,13},{9,17},{1... | collective-permute-start | bytes 614408 | tf_op jit(solution)/shard_map/ppermute | solution.py:438
  40.1 7.7 %collective-permute-start.5 = (s16[16,6400]{1,0:T(8,128)(2,1)S(1)}, s16[16,6400]{1,0:T(8,128)(2,1)S(1)}, u32[]{:S(2)}, u32[]{:S(2)}) collective-permute-start(s16[16,6400]{1,0:T(8,128)(2,1)S(1)} %get-tuple-element.17), channel_id=1, source_target_pairs={{8,0},{12,4},{16,8},{20,12},{24,16},{28,20},{9,1},{13,5},{17,9},{2... | collective-permute-start | bytes 614408 | tf_op jit(solution)/shard_map/ppermute | solution.py:437
  41.4 1.5 %copy-start.1 = (f32[8,2,8,3328]{3,2,1,0:T(8,128)S(1)}, f32[8,2,8,3328]{3,2,1,0:T(8,128)}, u32[]{:S(2)}) copy-start(f32[8,2,8,3328]{3,2,1,0:T(8,128)} %get-tuple-element.13.new_in_ref) | copy-start | bytes 5111812
  44.4 1.2 %copy-start.2 = (f32[8,2,8,3328]{3,2,1,0:T(8,128)}, f32[8,2,8,3328]{3,2,1,0:T(8,128)S(1)}, u32[]{:S(2)}) copy-start(f32[8,2,8,3328]{3,2,1,0:T(8,128)S(1)} %smooth.1.new_ref) | copy-start | bytes 5111812
  59.4 15.9 %copy-start.7 = (f32[64,64]{1,0:T(8,128)S(1)}, f32[64,64]{1,0:T(8,128)}, u32[]{:S(2)}) copy-start(f32[64,64]{1,0:T(8,128)} %remap_ref.1) | copy-start | bytes 49156
  59.4 15.9 %copy-start.8 = (bf16[64,192]{1,0:T(8,128)(2,1)S(1)}, bf16[64,192]{1,0:T(8,128)(2,1)}, u32[]{:S(2)}) copy-start(bf16[64,192]{1,0:T(8,128)(2,1)} %constant.37.clone.upward_ref) | copy-start | bytes 73732
  59.4 15.9 %all-to-all-start = ((s16[8,16,3200]{2,1,0:T(8,128)(2,1)}), s16[8,16,3200]{2,1,0:T(8,128)(2,1)S(1)}, u32[]{:S(2)}, u32[]{:S(2)}) async-start(s16[8,16,3200]{2,1,0:T(8,128)(2,1)} %second.1), calls=%async_computation | async-start | bytes 1638400 | tf_op jit(solution)/shard_map/all_to_all | solution.py:467
where the time goes:
time: 78.9 us; the launch traced here: 78.5 us
  Pallas kernels  28.6 us (36%)
  waiting for transfers between devices  26.3 us (33%)
  starting transfers between devices  17.6 us (22%)
  local copies, waits for them, and re-layouts  5.24 us (7%)
    all_to_all x1, waiting for transfers between devices, shards(): lax.all_to_all(codes, ('lat', 'lev'), 0, 0, axis_index_groups=groups, til...  12 us
    pallas_call x1, Pallas kernels, shards(): pl.pallas_call(functools.partial(second_kernel, z, parts), name='second',...  11.7 us
    pallas_call x1, Pallas kernels, shards(): pl.pallas_call(functools.partial(first_kernel, z), name='first', in_specs...  11.1 us
    ppermute x1, waiting for transfers between devices, shards(): edge = lax.ppermute(edge, 'lat', swap)  6.38 us
    ppermute x1, waiting for transfers between devices, shards(): inner = lax.ppermute(inner, 'lat', swap)  5.81 us
    unnamed x20, local copies, waits for them, and re-layouts  5.23 us
    ppermute x1, starting transfers between devices, shards(): far = lax.ppermute(edge, 'lat', far_pairs)  4.05 us
    all_to_all x1, starting transfers between devices, shards(): lax.all_to_all(codes, ('lat', 'lev'), 0, 0, axis_index_groups=groups, til...  3.85 us
  transfers between devices with their start and end apart: 7, of which 4 were waited for; matrix products, arithmetic and copies ran while one was open for 0% of the time, Pallas kernels for 2%

commit v1 on v0

--- a/solution.py
+++ b/solution.py
@@ -17,7 +17,7 @@
 TINY = 2.0**-100
 WIND = 81920.0
 ROUND = 1.5 * 2.0**23
-VMEM_LIMIT = 48 * 2**20
+VMEM_LIMIT = 32 * 2**20
 
 
 def rounded(values):
@@ -111,38 +111,62 @@
         inner_ref[:, at + i * z.lon : at + (i + 1) * z.lon] = wind_row(row, 1 - p)
 
 
-def substep(z, u_ref, fwx_ref, fwy_ref, write):
-    width = next(w for w in (768, 512, 384, 256, 128) if z.lon % w == 0)
-    wide = width + 2 * LANE
+def shifted(pieces, shift, lanes):
+    turned = [pltpu.roll(v, (-shift) % LANE, 1) for v in pieces]
+    if shift > 0:
+        return [jnp.where(lanes < LANE - shift, a, b) for a, b in zip(turned[1:-1], turned[2:])]
+    return [jnp.where(lanes < -shift, a, b) for a, b in zip(turned[:-2], turned[1:-1])]
+
+
+def substep(z, row_of, fwx_ref, fwm_ref, fwy_ref, write):
+    count = next(n for n in (4, 3, 2, 1) if z.lon % (n * LANE) == 0)
+    width = count * LANE
+    lanes = lax.broadcasted_iota(jnp.int32, (z.half, LANE), 1)
 
     def part(i, carry):
         at = pl.multiple_of(i * width, LANE)
-        mid = pl.multiple_of(at + LANE, LANE)
+
+        def piece(k):
+            return pl.ds(pl.multiple_of(at + k * LANE, LANE), LANE)
+
+        def row(j, f):
+            return [row_of(j, f, piece(k + 1)) for k in range(count)]
+
+        def start(j, f):
+            pieces = [row_of(j + 2, f, piece(k)) for k in range(count + 2)]
+            return [shifted(pieces, s, lanes) for s in (-2, -1, 1, 2)]
+
+        def lon_part(j, u, moved):
+            out = []
+            for k in range(count):
+                m2, m1, p1, p2 = (m[k] for m in moved)
+                east = 7.0 * (u[k] + p1) - (m1 + p2)
+                west = 7.0 * (m1 + u[k]) - (m2 + p1)
+                out.append(fwx_ref[j, :, piece(k)] * east - fwm_ref[j, :, piece(k)] * west)
+            return out
+
         for f in range(2):
-
-            def middle(j):
-                return u_ref[j, f, :, pl.ds(mid, width)]
-
-            rows = [middle(j) for j in range(4)]
-            sums = [rows[0] + rows[1], rows[1] + rows[2], rows[2] + rows[3]]
+            rows = [row(j, f) for j in range(4)]
+            sums = [[a + b for a, b in zip(rows[j], rows[j + 1])] for j in range(3)]
             flux = None
+            moved = start(0, f)
             for j in range(z.band + 1):
-                face = fwy_ref[j, :, pl.ds(at, width)]
-                new = face * (8.0 * sums[1] - (sums[0] + sums[2]))
+                later = start(j, f) if 0 < j < z.band else None
+                new = [
+                    fwy_ref[j, :, piece(k)] * (8.0 * sums[1][k] - (sums[0][k] + sums[2][k]))
+                    for k in range(count)
+                ]
                 if j > 0:
-                    u = u_ref[j + 1, f, :, pl.ds(at, wide)]
-                    pair = u + pltpu.roll(u, wide - 1, 1)
-                    high = pltpu.roll(pair, wide - 1, 1)
-                    low = pltpu.roll(pair, 1, 1)
-                    fx = fwx_ref[j - 1, :, pl.ds(at, wide)] * (8.0 * pair - (low + high))
-                    change = fx - pltpu.roll(fx, 1, 1)
-                    out = u[:, LANE : LANE + width] - change[:, LANE : LANE + width] - (new - flux)
-                    write(j - 1, f, at, width, out)
+                    u = rows[1]
+                    change = lon_part(j - 1, u, moved)
+                    for k in range(count):
+                        write(j - 1, f, at, k, u[k] - change[k] - (new[k] - flux[k]))
+                    moved = later
                 flux = new
                 if j < z.band:
-                    above = middle(j + 4)
+                    above = row(j + 4, f)
                     rows = rows[1:] + [above]
-                    sums = sums[1:] + [rows[2] + rows[3]]
+                    sums = sums[1:] + [[a + b for a, b in zip(rows[2], rows[3])]]
         return carry
 
     lax.fori_loop(0, z.lon // width, part, 0)
@@ -197,7 +221,7 @@
     return [smooth[i * tall : (i + 1) * tall].reshape(2, z.half, z.lon) for i in range(count)]
 
 
-def filter_band(z, cut_ref, first_row, forward_ref, back_ref, load, store):
+def filter_band(z, cut_ref, first_row, tables, load, store):
     nyquist = z.lon // 2
     for part in range(2):
         start = part * z.rows
@@ -207,7 +231,7 @@
         @pl.when(some)
         def _():
             rows = [load(start + r) for r in range(z.rows)]
-            smooth = low_pass(z, rows, cuts, forward_ref, back_ref)
+            smooth = low_pass(z, rows, cuts, *tables)
             for r in range(z.rows):
 
                 @pl.when(cuts[r] < nyquist)
@@ -217,7 +241,7 @@
 
 def first_kernel(
     z, par_ref, fields_ref, courant_ref, edge_ref, inner_ref, near_ref, far_ref,
-    new_ref, fwx_ref, fwy_ref, down_ref, up_ref, u_ref, cx_ref, cy_ref,
+    new_ref, fwx_ref, fwm_ref, fwy_ref, down_ref, up_ref, u_ref, cx_ref, cy_ref,
 ):
     p = par_ref[0]
     lon, half = z.lon, z.half
@@ -256,8 +280,10 @@
     cy_ref[9 * p] = winds(far_ref, at)[1]
 
     def face_rows(j, carry):
-        wind = cx_ref[j]
-        fwx_ref[j] = (wind + pltpu.roll(wind, z.pad - 1, 1)) * (1.0 / 24.0)
+        wind = cx_ref[j] * (1.0 / 24.0)
+        here = wind[:, LANE : LANE + lon]
+        fwx_ref[j] = here + pltpu.roll(wind, z.pad - 1, 1)[:, LANE : LANE + lon]
+        fwm_ref[j] = here + pltpu.roll(wind, 1, 1)[:, LANE : LANE + lon]
         return carry
 
     lax.fori_loop(0, z.band, face_rows, 0)
@@ -268,10 +294,10 @@
 
     lax.fori_loop(0, z.band + 1, face_cols, 0)
 
-    def write(row, f, at, width, values):
-        new_ref[row, f, :, pl.ds(pl.multiple_of(at + LANE, LANE), width)] = values
-
-    substep(z, u_ref, fwx_ref, fwy_ref, write)
+    def write(row, f, at, k, values):
+        new_ref[row, f, :, pl.ds(pl.multiple_of(at + (k + 1) * LANE, LANE), LANE)] = values
+
+    substep(z, lambda j, f, piece: u_ref[j, f, :, piece], fwx_ref, fwm_ref, fwy_ref, write)
     for r in range(2):
         for row, out_ref in ((r, down_ref), (z.band - 2 + r, up_ref)):
             values = new_ref[row, :, :, LANE : LANE + lon]
@@ -285,48 +311,66 @@
     lax.fori_loop(0, z.band, wrap, 0)
 
 
-def filter_kernel(z, par_ref, cut_ref, forward_ref, back_ref, new_in_ref, new_ref):
-    del new_in_ref
-    first_row = par_ref[1]
+def table_copies(forward_ref, back_ref, tables, sems):
+    refs = ((forward_ref, tables[0]), (back_ref, tables[1]))
+    return [pltpu.make_async_copy(a, b, sems.at[i]) for i, (a, b) in enumerate(refs)]
+
+
+def filter_kernel(
+    z, par_ref, cut_ref, forward_ref, back_ref, in_ref, new_ref, forward_copy, back_copy, sems
+):
+    tables = (forward_copy, back_copy)
+    copies = table_copies(forward_ref, back_ref, tables, sems)
+    for copy in copies:
+        copy.start()
+
+    def keep(j, carry):
+        new_ref[j] = in_ref[j]
+        return carry
+
+    lax.fori_loop(0, z.band, keep, 0)
+    for copy in copies:
+        copy.wait()
 
     def store(row, values):
         put_padded(new_ref, (row,), values, z.lon)
 
     filter_band(
-        z, cut_ref, first_row, forward_ref, back_ref,
-        lambda row: new_ref[row, :, :, LANE : LANE + z.lon], store,
+        z, cut_ref, par_ref[1], tables, lambda row: in_ref[row, :, :, LANE : LANE + z.lon], store
     )
 
 
 def second_kernel(
-    z, parts, par_ref, cut_ref, new_ref, fwx_ref, fwy_ref, below_ref, above_ref, forward_ref,
-    back_ref, out_ref, u_ref, v_ref,
+    z, parts, par_ref, cut_ref, new_ref, fwx_ref, fwm_ref, fwy_ref, below_ref, above_ref, forward_ref,
+    back_ref, out_ref, halo_ref, v_ref, forward_copy, back_copy, sems,
 ):
-    first_row = par_ref[1]
+    tables = (forward_copy, back_copy)
+    copies = table_copies(forward_ref, back_ref, tables, sems)
+    for copy in copies:
+        copy.start()
     lon, half = z.lon, z.half
     tall = 2 * half
     for r in range(2):
-        for row, in_ref in ((r, below_ref), (z.band + 2 + r, above_ref)):
-            values = decode_row(in_ref, r * z.code, lon).reshape(2, half, lon)
-            put_padded(u_ref, (row,), values, lon)
-
-    def copy(j, carry):
-        u_ref[j + 2] = new_ref[j]
-        return carry
-
-    lax.fori_loop(0, z.band, copy, 0)
-
-    def write(row, f, at, width, values):
-        v_ref[row, f, :, pl.ds(at, width)] = values
-
-    substep(z, u_ref, fwx_ref, fwy_ref, write)
+        for row, in_ref in ((r, below_ref), (2 + r, above_ref)):
+            halo_ref[row] = decode_row(in_ref, r * z.code, lon).reshape(2, half, lon)
+
+    def row_of(j, f, piece):
+        if 2 <= j < z.band + 2:
+            return new_ref[j - 2, f, :, piece]
+        start = pl.multiple_of(piece.start - LANE, LANE)
+        return halo_ref[j if j < 2 else j - z.band, f, :, pl.ds(start, LANE)]
+
+    def write(row, f, at, k, values):
+        v_ref[row, f, :, pl.ds(pl.multiple_of(at + k * LANE, LANE), LANE)] = values
+
+    substep(z, row_of, fwx_ref, fwm_ref, fwy_ref, write)
 
     def store(row, values):
         v_ref[row] = values
 
-    filter_band(
-        z, cut_ref, first_row, forward_ref, back_ref, lambda row: v_ref[row], store
-    )
+    for copy in copies:
+        copy.wait()
+    filter_band(z, cut_ref, par_ref[1], tables, lambda row: v_ref[row], store)
     column = lon // parts
     for side in range(2):
         for d in range(parts):
@@ -373,6 +417,10 @@
     return pl.BlockSpec(memory_space=pltpu.SMEM)
 
 
+def far_memory():
+    return pl.BlockSpec(memory_space=pltpu.HBM)
+
+
 def params():
     return pltpu.CompilerParams(vmem_limit_bytes=VMEM_LIMIT)
 
@@ -414,14 +462,15 @@
     inner = lax.ppermute(inner, "lat", swap)
     far = lax.ppermute(edge, "lat", far_pairs)
 
-    new, fwx, fwy, down, up = pl.pallas_call(
+    new, fwx, fwm, fwy, down, up = pl.pallas_call(
         functools.partial(first_kernel, z),
         name="first",
         in_specs=[scalars()] + [whole()] * 6,
-        out_specs=[whole()] * 5,
+        out_specs=[whole()] * 6,
         out_shape=[
             jax.ShapeDtypeStruct((z.band, 2, z.half, z.pad), f32),
-            jax.ShapeDtypeStruct((z.band, z.half, z.pad), f32),
+            jax.ShapeDtypeStruct((z.band, z.half, z.lon), f32),
+            jax.ShapeDtypeStruct((z.band, z.half, z.lon), f32),
             jax.ShapeDtypeStruct((z.band + 1, z.half, z.lon), f32),
             jax.ShapeDtypeStruct((tall, 2 * z.code), i16),
             jax.ShapeDtypeStruct((tall, 2 * z.code), i16),
@@ -438,13 +487,15 @@
     below = lax.ppermute(up, "lat", rising)
 
     forward, back = (jnp.asarray(t) for t in filter_tables(lon))
+    table_scratch = [pltpu.VMEM(t.shape, t.dtype) for t in (forward, back)]
+    table_scratch.append(pltpu.SemaphoreType.DMA((2,)))
     new = pl.pallas_call(
         functools.partial(filter_kernel, z),
         name="smooth",
-        in_specs=[scalars(), scalars()] + [whole()] * 3,
+        in_specs=[scalars(), scalars(), far_memory(), far_memory(), whole()],
         out_specs=whole(),
         out_shape=jax.ShapeDtypeStruct(new.shape, f32),
-        input_output_aliases={4: 0},
+        scratch_shapes=table_scratch,
         compiler_params=params(),
         cost_estimate=cost(10**9, 6 * 10**6),
     )(place, cutoffs, forward, back, new)
@@ -453,16 +504,17 @@
     codes = pl.pallas_call(
         functools.partial(second_kernel, z, parts),
         name="second",
-        in_specs=[scalars(), scalars()] + [whole()] * 7,
+        in_specs=[scalars(), scalars()] + [whole()] * 6 + [far_memory()] * 2,
         out_specs=whole(),
         out_shape=jax.ShapeDtypeStruct((2 * parts, tall, rows * column + LANE), i16),
         scratch_shapes=[
-            pltpu.VMEM((z.band + 4, 2, z.half, z.pad), f32),
+            pltpu.VMEM((4, 2, z.half, lon), f32),
             pltpu.VMEM((z.band, 2, z.half, lon), f32),
-        ],
+        ]
+        + table_scratch,
         compiler_params=params(),
         cost_estimate=cost(10**9, 8 * 10**6),
-    )(place, cutoffs, new, fwx, fwy, below, above, forward, back)
+    )(place, cutoffs, new, fwx, fwm, fwy, below, above, forward, back)
     groups = [[i * parts + j for i in (a, a + 1) for j in range(parts)] for a in range(0, lats, 2)]
     got = lax.all_to_all(codes, ("lat", "lev"), 0, 0, axis_index_groups=groups, tiled=True)
 

time: 78.9 us -> 66.4 us (0.84)
  Pallas kernels: 28.6 us -> 16.6 us
  local copies, waits for them, and re-layouts: 5.24 us -> 2.59 us
  waiting for transfers between devices: 26.3 us -> 28.6 us
    pallas_call x1, Pallas kernels: 11.1 us -> 4.8 us  [shards(): pl.pallas_call(functools.partial(first_kernel, z), name='first', in_specs...]
    pallas_call x1, Pallas kernels: 11.7 us -> 5.57 us  [shards(): pl.pallas_call(functools.partial(second_kernel, z, parts), name='second',...]
    unnamed x20 -> x16, local copies, waits for them, and re-layouts: 5.23 us -> 2.57 us
    ppermute x1, waiting for transfers between devices: 2.12 us -> 4.22 us  [shards(): above = lax.ppermute(down, 'lat', falling)]
  transfers between devices with their start and end apart: 7 -> 7, of which waited for: 4 -> 5; matrix products, arithmetic and copies ran while one was open for 0% -> 0% of each run, Pallas kernels for 2% -> 3%
where the time goes in v1:
time: 66.4 us; the launch traced here: 66.1 us
  waiting for transfers between devices  28.6 us (43%)
  starting transfers between devices  17.4 us (26%)
  Pallas kernels  16.6 us (25%)
  local copies, waits for them, and re-layouts  2.59 us (4%)
  between operations  0.79 us (1%)
    all_to_all x1, waiting for transfers between devices, shards(): lax.all_to_all(codes, ('lat', 'lev'), 0, 0, axis_index_groups=groups, til...  12 us
    ppermute x1, waiting for transfers between devices, shards(): edge = lax.ppermute(edge, 'lat', swap)  6.38 us
    ppermute x1, waiting for transfers between devices, shards(): inner = lax.ppermute(inner, 'lat', swap)  5.81 us
    pallas_call x1, Pallas kernels, shards(): pl.pallas_call(functools.partial(second_kernel, z, parts), name='second',...  5.57 us
    pallas_call x1, Pallas kernels, shards(): pl.pallas_call(functools.partial(first_kernel, z), name='first', in_specs...  4.8 us
    ppermute x1, waiting for transfers between devices, shards(): above = lax.ppermute(down, 'lat', falling)  4.22 us
    ppermute x1, starting transfers between devices, shards(): far = lax.ppermute(edge, 'lat', far_pairs)  4.05 us
    ppermute x1, starting transfers between devices, shards(): below = lax.ppermute(up, 'lat', rising)  3.74 us
  transfers between devices with their start and end apart: 7, of which 5 were waited for; matrix products, arithmetic and copies ran while one was open for 0% of the time, Pallas kernels for 3%

profile of v1, /device:TPU:0, one launch (start us, length us, event | category | flops | bytes accessed | tf_op | source)
XLA Modules:
  0.0 66.1 jit_solution(2735825139068974748)
XLA Ops:
  0.6 0.0 copy-start
  0.7 0.1 pad_add_fusion.par_ref
  0.7 0.0 copy-start.3
  0.7 1.4 %copy-done.3 = f32[2,4,16,3072]{3,2,1,0:T(8,128)S(1)} copy-done((f32[2,4,16,3072]{3,2,1,0:T(8,128)S(1)}, f32[2,4,16,3072]{3,2,1,0:T(8,128)}, u32[]{:S(2)}) %copy-start.3) | copy-done | bytes 1572888
  2.1 0.0 copy-start.4
  2.1 1.1 %copy-done.4 = bf16[2,4,16,3072]{3,2,1,0:T(8,128)(2,1)S(1)} copy-done((bf16[2,4,16,3072]{3,2,1,0:T(8,128)(2,1)S(1)}, bf16[2,4,16,3072]{3,2,1,0:T(8,128)(2,1)}, u32[]{:S(2)}) %copy-start.4) | copy-done | bytes 786456
  3.3 1.1 %pack.1 = (s16[16,9472]{1,0:T(8,128)(2,1)S(1)}, s16[16,15616]{1,0:T(8,128)(2,1)S(1)}, s16[16,9472]{1,0:T(8,128)(2,1)S(1)}) custom-call(s32[2]{0:T(128)S(1)} %pad_add_fusion.par_ref, f32[2,4,16,3072]{3,2,1,0:T(8,128)S(1)} %copy-done.3, bf16[2,4,16,3072]{3,2,1,0:T(8,128)(2,1)S(1)} %copy-done.4), custom_call_target="tpu_custom_call" | custom-call | flops 10000000 | bytes 5000000 | tf_op jit(solution)/shard_map/pack/pallas_call | solution.py:447
  4.4 3.0 %collective-permute-start = (s16[16,9472]{1,0:T(8,128)(2,1)S(1)}, s16[16,9472]{1,0:T(8,128)(2,1)S(1)}, u32[]{:S(2)}, u32[]{:S(2)}) collective-permute-start(s16[16,9472]{1,0:T(8,128)(2,1)S(1)} %get-tuple-element.11), channel_id=1, source_target_pairs={{0,4},{4,0},{8,12},{12,8},{16,20},{20,16},{24,28},{28,24},{1,5},{5... | collective-permute-start | bytes 909320 | tf_op jit(solution)/shard_map/ppermute | solution.py:460
  7.4 0.1 collective-permute-start.1
  7.5 0.0 copy-start.1
  7.5 0.0 copy-start.2
  7.5 0.0 copy-start.7
  7.5 1.5 %collective-permute-start.2 = (s16[16,9472]{1,0:T(8,128)(2,1)S(1)}, s16[16,9472]{1,0:T(8,128)(2,1)S(1)}, u32[]{:S(2)}, u32[]{:S(2)}) collective-permute-start(s16[16,9472]{1,0:T(8,128)(2,1)S(1)} %get-tuple-element.13), channel_id=1, source_target_pairs={{4,12},{12,20},{20,28},{8,0},{16,8},{24,16},{5,13},{13,21},{21,29}... | collective-permute-start | bytes 909320 | tf_op jit(solution)/shard_map/ppermute | solution.py:461
  9.0 6.4 %collective-permute-done.edge_ref = s16[16,9472]{1,0:T(8,128)(2,1)S(1)} collective-permute-done((s16[16,9472]{1,0:T(8,128)(2,1)S(1)}, s16[16,9472]{1,0:T(8,128)(2,1)S(1)}, u32[]{:S(2)}, u32[]{:S(2)}) %collective-permute-start) | collective-permute-done | bytes 303136 | tf_op jit(solution)/shard_map/ppermute | solution.py:460
  15.4 4.1 %collective-permute-start.3 = (s16[16,9472]{1,0:T(8,128)(2,1)S(1)}, s16[16,9472]{1,0:T(8,128)(2,1)S(1)}, u32[]{:S(2)}, u32[]{:S(2)}) collective-permute-start(s16[16,9472]{1,0:T(8,128)(2,1)S(1)} %collective-permute-done.edge_ref), channel_id=1, source_target_pairs={{0,8},{8,16},{16,24},{12,4},{20,12},{28,20},{1,9},{9,17},{17,25},{... | collective-permute-start | bytes 909320 | tf_op jit(solution)/shard_map/ppermute | solution.py:463
  19.5 0.0 collective-permute-done.2.near_ref
  19.5 5.8 %collective-permute-done.1.inner_ref = s16[16,15616]{1,0:T(8,128)(2,1)S(1)} collective-permute-done((s16[16,15616]{1,0:T(8,128)(2,1)S(1)}, s16[16,15616]{1,0:T(8,128)(2,1)S(1)}, u32[]{:S(2)}, u32[]{:S(2)}) %collective-permute-start.1) | collective-permute-done | bytes 499744 | tf_op jit(solution)/shard_map/ppermute | solution.py:462
  25.3 0.0 collective-permute-done.3.far_ref
  25.3 4.8 %first.1 = (f32[8,2,8,3328]{3,2,1,0:T(8,128)S(1)}, f32[8,8,3072]{2,1,0:T(8,128)S(1)}, f32[8,8,3072]{2,1,0:T(8,128)S(1)}, f32[9,8,3072]{2,1,0:T(8,128)S(1)}, s16[...) custom-call(s32[2]{0:T(128)S(1)} %pad_add_fusion.par_ref, f32[2,4,16,3072]{3,2,1,0:T(8,128)S(1)} %copy-done.3, ...), custom_call_target="tpu_custom_call" | custom-call | flops 40000000 | bytes 8000000 | tf_op jit(solution)/shard_map/first/pallas_call | solution.py:465
  30.1 3.7 %collective-permute-start.4 = (s16[16,6400]{1,0:T(8,128)(2,1)S(1)}, s16[16,6400]{1,0:T(8,128)(2,1)S(1)}, u32[]{:S(2)}, u32[]{:S(2)}) collective-permute-start(s16[16,6400]{1,0:T(8,128)(2,1)S(1)} %get-tuple-element.18), channel_id=1, source_target_pairs={{0,8},{4,12},{8,16},{12,20},{16,24},{20,28},{1,9},{5,13},{9,17},{1... | collective-permute-start | bytes 614408 | tf_op jit(solution)/shard_map/ppermute | solution.py:487
  33.8 1.3 %collective-permute-start.5 = (s16[16,6400]{1,0:T(8,128)(2,1)S(1)}, s16[16,6400]{1,0:T(8,128)(2,1)S(1)}, u32[]{:S(2)}, u32[]{:S(2)}) collective-permute-start(s16[16,6400]{1,0:T(8,128)(2,1)S(1)} %get-tuple-element.19), channel_id=1, source_target_pairs={{8,0},{12,4},{16,8},{20,12},{24,16},{28,20},{9,1},{13,5},{17,9},{2... | collective-permute-start | bytes 614408 | tf_op jit(solution)/shard_map/ppermute | solution.py:486
  35.1 0.0 copy-done.1
  35.2 0.0 copy-done.2
  35.2 0.0 copy-done.7
  35.2 1.9 %smooth.1.new_ref = f32[8,2,8,3328]{3,2,1,0:T(8,128)S(1)} custom-call(s32[2]{0:T(128)S(1)} %pad_add_fusion.par_ref, s32[32]{0:T(128)S(1)} %copy-done.7, bf16[2,1536,256]{2,1,0:T(8,128)(2,1)S(1)} %copy-done.1, bf16[2,256,1536]{2,1,0:T(8,128)(2,1)S(1)} %copy-done.2, f32[8,2,8,3328]{3,2,1,0:T(8,128)S(1)} %get-tuple-element.14.in_ref), custom_call_target="tpu_custom_call" | custom-call | flops 1000000000 | bytes 6000000 | tf_op jit(solution)/shard_map/smooth/pallas_call | solution.py:492
  37.1 0.2 collective-permute-done.4.below_ref
  37.3 4.2 %collective-permute-done.5.above_ref = s16[16,6400]{1,0:T(8,128)(2,1)S(1)} collective-permute-done((s16[16,6400]{1,0:T(8,128)(2,1)S(1)}, s16[16,6400]{1,0:T(8,128)(2,1)S(1)}, u32[]{:S(2)}, u32[]{:S(2)}) %collective-permute-start.5) | collective-permute-done | bytes 204832 | tf_op jit(solution)/shard_map/ppermute | solution.py:486
  41.5 5.6 %second.1 = s16[8,16,3200]{2,1,0:T(8,128)(2,1)} custom-call(s32[2]{0:T(128)S(1)} %pad_add_fusion.par_ref, s32[32]{0:T(128)S(1)} %copy-done.7, f32[8,2,8,3328]{3,2,1,0:T(8,128)S(1)} %smooth.1.new_ref, f32[8,8,3072]{2,1,0:T(8,128)S(1)} %get-tuple-element.15.fwx_ref, f32[8,8,3072]{2,1,0:T(8,128)S(1)} %get-tuple-element.16.fwm_ref, ...), custom_call_target="tpu_custom_call" | custom-call | flops 1000000000 | bytes 8000000 | tf_op jit(solution)/shard_map/second/pallas_call | solution.py:504
  47.1 0.0 copy-start.5
  47.1 0.0 copy-start.6
  47.1 3.7 %all-to-all-start = ((s16[8,16,3200]{2,1,0:T(8,128)(2,1)}), s16[8,16,3200]{2,1,0:T(8,128)(2,1)S(1)}, u32[]{:S(2)}, u32[]{:S(2)}) async-start(s16[8,16,3200]{2,1,0:T(8,128)(2,1)} %second.1), calls=%async_computation | async-start | bytes 1638400 | tf_op jit(solution)/shard_map/all_to_all | solution.py:519
  50.8 0.0 copy-done
  50.9 12.0 %all-to-all-done.got_ref = s16[8,16,3200]{2,1,0:T(8,128)(2,1)S(1)} async-done(((s16[8,16,3200]{2,1,0:T(8,128)(2,1)}), s16[8,16,3200]{2,1,0:T(8,128)(2,1)S(1)}, u32[]{:S(2)}, u32[]{:S(2)}) %all-to-all-start) | async-done | bytes 819232 | tf_op jit(solution)/shard_map/all_to_all | solution.py:519
  62.8 0.0 copy-done.5
  62.8 0.0 copy-done.6
  62.8 3.2 %columns.1 = (f32[2,4,64,768]{3,2,1,0:T(8,128)}, f32[4,64,768]{2,1,0:T(8,128)}) custom-call(s32[2]{0:T(128)S(1)} %pad_add_fusion.par_ref, s16[8,16,3200]{2,1,0:T(8,128)(2,1)S(1)} %all-to-all-done.got_ref, f32[64,64]{1,0:T(8,128)S(1)} %copy-done.5, bf16[64,192]{1,0:T(8,128)(2,1)S(1)} %copy-done.6, f32[4,1,768]{2,1,0:T(1,128)S(1)} %broadcast_in_dim.3.surface_ref), custom_call_target="tpu_custom_call" | custom-call | flops 100000000 | bytes 4000000 | tf_op jit(solution)/shard_map/columns/pallas_call | solution.py:527
  (2 shorter events, 0.0 us)
Async XLA Ops:
  0.6 50.2 %copy-start = (f32[4,3072]{1,0:T(4,128)S(1)}, f32[4,3072]{1,0:T(4,128)}, u32[]{:S(2)}) copy-start(f32[4,3072]{1,0:T(4,128)} %param.11) | copy-start | bytes 147460
  0.7 1.4 %copy-start.3 = (f32[2,4,16,3072]{3,2,1,0:T(8,128)S(1)}, f32[2,4,16,3072]{3,2,1,0:T(8,128)}, u32[]{:S(2)}) copy-start(f32[2,4,16,3072]{3,2,1,0:T(8,128)} %fields_ref.3) | copy-start | bytes 4718596
  2.1 1.1 %copy-start.4 = (bf16[2,4,16,3072]{3,2,1,0:T(8,128)(2,1)S(1)}, bf16[2,4,16,3072]{3,2,1,0:T(8,128)(2,1)}, u32[]{:S(2)}) copy-start(bf16[2,4,16,3072]{3,2,1,0:T(8,128)(2,1)} %courant_ref.3) | copy-start | bytes 2359300
  4.4 11.0 %collective-permute-start = (s16[16,9472]{1,0:T(8,128)(2,1)S(1)}, s16[16,9472]{1,0:T(8,128)(2,1)S(1)}, u32[]{:S(2)}, u32[]{:S(2)}) collective-permute-start(s16[16,9472]{1,0:T(8,128)(2,1)S(1)} %get-tuple-element.11), channel_id=1, source_target_pairs={{0,4},{4,0},{8,12},{12,8},{16,20},{20,16},{24,28},{28,24},{1,5},{5... | collective-permute-start | bytes 909320 | tf_op jit(solution)/shard_map/ppermute | solution.py:460
  7.4 17.9 %collective-permute-start.1 = (s16[16,15616]{1,0:T(8,128)(2,1)S(1)}, s16[16,15616]{1,0:T(8,128)(2,1)S(1)}, u32[]{:S(2)}, u32[]{:S(2)}) collective-permute-start(s16[16,15616]{1,0:T(8,128)(2,1)S(1)} %get-tuple-element.12), channel_id=1, source_target_pairs={{0,4},{4,0},{8,12},{12,8},{16,20},{20,16},{24,28},{28,24},{1,5},{5... | collective-permute-start | bytes 1499144 | tf_op jit(solution)/shard_map/ppermute | solution.py:462
  7.5 27.7 %copy-start.1 = (bf16[2,1536,256]{2,1,0:T(8,128)(2,1)S(1)}, bf16[2,1536,256]{2,1,0:T(8,128)(2,1)}, u32[]{:S(2)}) copy-start(bf16[2,1536,256]{2,1,0:T(8,128)(2,1)} %constant.35.clone.forward_ref) | copy-start | bytes 4718596
  7.5 27.7 %copy-start.2 = (bf16[2,256,1536]{2,1,0:T(8,128)(2,1)S(1)}, bf16[2,256,1536]{2,1,0:T(8,128)(2,1)}, u32[]{:S(2)}) copy-start(bf16[2,256,1536]{2,1,0:T(8,128)(2,1)} %constant.36.clone.back_ref) | copy-start | bytes 4718596
  7.5 27.7 %copy-start.7 = (s32[32]{0:T(128)S(1)}, s32[32]{0:T(128)}, u32[]{:S(2)}) copy-start(s32[32]{0:T(128)} %cut_ref.3) | copy-start | bytes 388
  7.5 12.0 %collective-permute-start.2 = (s16[16,9472]{1,0:T(8,128)(2,1)S(1)}, s16[16,9472]{1,0:T(8,128)(2,1)S(1)}, u32[]{:S(2)}, u32[]{:S(2)}) collective-permute-start(s16[16,9472]{1,0:T(8,128)(2,1)S(1)} %get-tuple-element.13), channel_id=1, source_target_pairs={{4,12},{12,20},{20,28},{8,0},{16,8},{24,16},{5,13},{13,21},{21,29}... | collective-permute-start | bytes 909320 | tf_op jit(solution)/shard_map/ppermute | solution.py:461
  15.4 9.9 %collective-permute-start.3 = (s16[16,9472]{1,0:T(8,128)(2,1)S(1)}, s16[16,9472]{1,0:T(8,128)(2,1)S(1)}, u32[]{:S(2)}, u32[]{:S(2)}) collective-permute-start(s16[16,9472]{1,0:T(8,128)(2,1)S(1)} %collective-permute-done.edge_ref), channel_id=1, source_target_pairs={{0,8},{8,16},{16,24},{12,4},{20,12},{28,20},{1,9},{9,17},{17,25},{... | collective-permute-start | bytes 909320 | tf_op jit(solution)/shard_map/ppermute | solution.py:463
  30.1 7.2 %collective-permute-start.4 = (s16[16,6400]{1,0:T(8,128)(2,1)S(1)}, s16[16,6400]{1,0:T(8,128)(2,1)S(1)}, u32[]{:S(2)}, u32[]{:S(2)}) collective-permute-start(s16[16,6400]{1,0:T(8,128)(2,1)S(1)} %get-tuple-element.18), channel_id=1, source_target_pairs={{0,8},{4,12},{8,16},{12,20},{16,24},{20,28},{1,9},{5,13},{9,17},{1... | collective-permute-start | bytes 614408 | tf_op jit(solution)/shard_map/ppermute | solution.py:487
  33.8 7.7 %collective-permute-start.5 = (s16[16,6400]{1,0:T(8,128)(2,1)S(1)}, s16[16,6400]{1,0:T(8,128)(2,1)S(1)}, u32[]{:S(2)}, u32[]{:S(2)}) collective-permute-start(s16[16,6400]{1,0:T(8,128)(2,1)S(1)} %get-tuple-element.19), channel_id=1, source_target_pairs={{8,0},{12,4},{16,8},{20,12},{24,16},{28,20},{9,1},{13,5},{17,9},{2... | collective-permute-start | bytes 614408 | tf_op jit(solution)/shard_map/ppermute | solution.py:486
  47.1 15.8 %copy-start.5 = (f32[64,64]{1,0:T(8,128)S(1)}, f32[64,64]{1,0:T(8,128)}, u32[]{:S(2)}) copy-start(f32[64,64]{1,0:T(8,128)} %remap_ref.1) | copy-start | bytes 49156
  47.1 15.8 %copy-start.6 = (bf16[64,192]{1,0:T(8,128)(2,1)S(1)}, bf16[64,192]{1,0:T(8,128)(2,1)}, u32[]{:S(2)}) copy-start(bf16[64,192]{1,0:T(8,128)(2,1)} %constant.37.clone.upward_ref) | copy-start | bytes 73732
  47.1 15.7 %all-to-all-start = ((s16[8,16,3200]{2,1,0:T(8,128)(2,1)}), s16[8,16,3200]{2,1,0:T(8,128)(2,1)S(1)}, u32[]{:S(2)}, u32[]{:S(2)}) async-start(s16[8,16,3200]{2,1,0:T(8,128)(2,1)} %second.1), calls=%async_computation | async-start | bytes 1638400 | tf_op jit(solution)/shard_map/all_to_all | solution.py:519
